TPU v7x, 32 devices: a whole 2x2x4 slice. The times are simulated.
32 devices in a mesh: rx: 8 (over y, x, core), ry: 4 (over z).
Axes of the slice: x: 2, y: 2, z: 4, core: 2. Of those that a mesh axis runs over, the one named last changes fastest.
Arguments:
- rhs: float32 [4096, 128], P(('rx', 'ry')), may hold values from -6 to 6
- a_diag: bfloat16 [4096, 128, 128], P(('rx', 'ry'))
- a_pair: bfloat16 [4096, 128, 128], P(('rx', 'ry')), may hold values from -0.25 to 0.25
- a_far: bfloat16 [4096, 2, 128, 128], P(('rx', 'ry')), may hold values from -0.25 to 0.25
- approx_inv: bfloat16 [4096, 128, 128], P(('rx', 'ry'))
- prolong: bfloat16 [4096, 128, 128], P(('rx', 'ry'))
- col_index: int32 [4096, 2], P(('rx', 'ry')), may hold values from 0 to 4095, as said below
- partner: int32 [2048], P(('rx', 'ry')), may hold values from 1 to 4095, as said below
- odd_owner: int32 [2048], P(('rx', 'ry')), may hold values from 0 to 2047, as said below
Outputs:
- fine: float32 [4096, 128], P(('rx', 'ry'))
- coarse_blocks: bfloat16 [2048, 128, 128], P(('rx', 'ry'))
- coarse_residual: float32 [2048, 128], P(('rx', 'ry'))
Inputs may be any that keep to these rules, and one draw needn't show every extreme that they name: partner[c] is an odd fine row on another device with the same ry index as coarse row c's device (coarse row c stands on device c // 64, fine row i on device i // 128); every odd fine row is named once; the odd rows of each device go to exactly 4 devices, 16 rows to each. odd_owner[o] is the coarse row c with partner[c] = 2o + 1. col_index[i,0] is a block row of a device with the same ry index as row i's device; col_index[i,1] a block row of the device with the same rx index whose ry index is one more or one less, wrapping.
All inputs are finite; a program needn't handle non-finite values.
Results may differ from a plain program's by a relative error of at most 0.0065.
Values may be sent and summed in bfloat16 or wider, within the bound.
A program may use at most 128 MiB of HBM per device.

v0:
```python
import jax
import jax.numpy as jnp
from jax import lax
from jax.sharding import PartitionSpec as P

OMEGA = 0.7
THETA = 0.08


def for_sending(shard):
    return jax.tree.map(lambda a: a.astype(jnp.bfloat16) if a.dtype == jnp.float32 else a, shard)


def with_halo(block, sides, width):
    for axis, dim in sides:
        count = lax.axis_size(axis)
        forward = [(i, i + 1) for i in range(count - 1)]
        forward.append((count - 1, 0))
        backward = [(target, source) for source, target in forward]
        low = lax.ppermute(
            lax.slice_in_dim(block, block.shape[dim] - width, None, axis=dim), axis, forward
        )
        high = lax.ppermute(lax.slice_in_dim(block, 0, width, axis=dim), axis, backward)
        block = jnp.concatenate([low, block, high], axis=dim)
    return block


def mat_vec(matrix, vector):
    return jnp.einsum(
        "nij,nj->ni", matrix.astype(jnp.float32), vector, precision=lax.Precision.HIGHEST
    )


def mat_tvec(matrix, vector):
    return jnp.einsum(
        "nji,nj->ni", matrix.astype(jnp.float32), vector, precision=lax.Precision.HIGHEST
    )


def left_product(left_mat, right_mat):
    return jnp.einsum("nji,njk->nik", left_mat, right_mat, preferred_element_type=jnp.float32)


def plain_product(left_mat, right_mat):
    return jnp.einsum("nij,njk->nik", left_mat, right_mat, preferred_element_type=jnp.float32)


def slot_table(lines, ranks, line_size, capacity):
    peer_ids = jnp.arange(line_size, dtype=jnp.int32)[:, None, None]
    rank_ids = jnp.arange(capacity, dtype=jnp.int32)[None, :, None]
    hits = (lines[None, None, :] == peer_ids) & (ranks[None, None, :] == rank_ids)
    item_ids = jnp.arange(lines.shape[0], dtype=jnp.int32)[None, None, :]
    chosen = jnp.sum(jnp.where(hits, item_ids, 0), axis=2).reshape(-1)
    filled = jnp.any(hits, axis=2).reshape(-1)
    return (chosen, filled)


def pack_slots(values, chosen, filled, line_size, capacity):
    taken = values[chosen]
    mask = filled.reshape((-1,) + (1,) * (values.ndim - 1))
    taken = jnp.where(mask, taken, jnp.zeros_like(taken))
    return taken.reshape((line_size, capacity) + values.shape[1:])


def body(rhs, a_diag, a_pair, a_far, approx_inv, prolong, col_index, partner, odd_owner):
    row_count = rhs.shape[0]
    half_rows = row_count // 2
    line_size = lax.axis_size("rx")
    side_size = lax.axis_size("ry")
    side_pos = lax.axis_index("ry")
    capacity = half_rows // (line_size // 2)
    mate = jnp.stack([partner, 2 * odd_owner], axis=1).reshape(row_count)

    def line_slot(global_row):
        return global_row // row_count // side_size * row_count + global_row % row_count

    mate_slot = line_slot(mate)
    far_slot = line_slot(col_index[:, 0])
    side_dev = col_index[:, 1] // row_count
    below = side_dev % side_size == (side_pos - 1) % side_size
    side_slot = jnp.where(below, 0, 2 * row_count) + col_index[:, 1] % row_count

    def operate(vector):
        whole_line = lax.all_gather(vector, "rx", axis=0, tiled=True)
        mate_vals = whole_line[mate_slot]
        far_vals = whole_line[far_slot]
        sides = with_halo(for_sending(vector[None]), (("ry", 0),), 1).reshape(
            3 * row_count, vector.shape[1]
        )
        total = mat_vec(a_diag, vector) + mat_vec(a_pair, mate_vals)
        total = total + mat_vec(a_far[:, 0], far_vals)
        return total + mat_vec(a_far[:, 1], sides[side_slot])

    iterate = OMEGA * mat_vec(approx_inv, rhs)
    iterate = iterate + OMEGA * mat_vec(approx_inv, rhs - operate(iterate))
    residual = rhs - operate(iterate)
    odd_prol = prolong[1::2]
    lower = left_product(odd_prol, a_diag[1::2]).astype(jnp.bfloat16)
    inner = plain_product(lower, odd_prol).astype(jnp.bfloat16)
    behind = left_product(odd_prol, a_pair[1::2]).astype(jnp.bfloat16)
    odd_piece = mat_tvec(odd_prol, residual[1::2])
    target_line = odd_owner // half_rows // side_size
    same_target = target_line[:, None] == target_line[None, :]
    earlier = odd_owner[None, :] < odd_owner[:, None]
    send_rank = jnp.sum(same_target & earlier, axis=1)
    send_items, send_filled = slot_table(target_line, send_rank, line_size, capacity)
    source_line = partner // row_count // side_size
    same_source = source_line[:, None] == source_line[None, :]
    position = jnp.arange(half_rows, dtype=jnp.int32)
    before = position[None, :] < position[:, None]
    recv_rank = jnp.sum(same_source & before, axis=1)
    recv_slot = source_line * capacity + recv_rank

    def unpack(received):
        return received.reshape((line_size * capacity,) + received.shape[2:])[recv_slot]

    sent_prol, sent_behind, sent_inner = (
        lax.all_to_all(
            pack_slots(odd_prol, send_items, send_filled, line_size, capacity),
            "rx",
            split_axis=0,
            concat_axis=0,
            tiled=True,
        ),
        lax.all_to_all(
            pack_slots(behind, send_items, send_filled, line_size, capacity),
            "rx",
            split_axis=0,
            concat_axis=0,
            tiled=True,
        ),
        lax.all_to_all(
            pack_slots(inner, send_items, send_filled, line_size, capacity),
            "rx",
            split_axis=0,
            concat_axis=0,
            tiled=True,
        ),
    )
    got_prol = unpack(sent_prol)
    got_behind = unpack(sent_behind)
    got_inner = unpack(sent_inner)
    got_piece = unpack(
        lax.all_to_all(
            for_sending(pack_slots(odd_piece, send_items, send_filled, line_size, capacity)),
            "rx",
            split_axis=0,
            concat_axis=0,
            tiled=True,
        )
    )
    even_prol = prolong[0::2]
    upper = left_product(even_prol, a_diag[0::2]).astype(jnp.bfloat16)
    across = left_product(even_prol, a_pair[0::2]).astype(jnp.bfloat16)
    total = plain_product(upper, even_prol) + plain_product(across, got_prol)
    total = total + plain_product(got_behind, even_prol) + got_inner.astype(jnp.float32)
    blocks = lax.optimization_barrier(total.astype(jnp.bfloat16))
    restricted = mat_tvec(even_prol, residual[0::2]) + got_piece
    correction = THETA * restricted
    correction = correction + THETA * (restricted - mat_vec(blocks, correction))
    lift_even = mat_vec(even_prol, correction)
    back_items, back_filled = slot_table(source_line, recv_rank, line_size, capacity)
    returned = lax.all_to_all(
        for_sending(pack_slots(correction, back_items, back_filled, line_size, capacity)),
        "rx",
        split_axis=0,
        concat_axis=0,
        tiled=True,
    )
    odd_correction = returned.reshape(line_size * capacity, returned.shape[2])[
        target_line * capacity + send_rank
    ]
    lift_odd = mat_vec(odd_prol, odd_correction)
    fine = jnp.stack([iterate[0::2] + lift_even, iterate[1::2] + lift_odd], axis=1).reshape(
        row_count, rhs.shape[1]
    )
    return (fine, blocks, restricted)


def solution(mesh):
    return jax.shard_map(
        body,
        mesh=mesh,
        in_specs=(
            P(("rx", "ry"), None),
            P(("rx", "ry"), None, None),
            P(("rx", "ry"), None, None),
            P(("rx", "ry"), None, None, None),
            P(("rx", "ry"), None, None),
            P(("rx", "ry"), None, None),
            P(("rx", "ry"), None),
            P(("rx", "ry")),
            P(("rx", "ry")),
        ),
        out_specs=(P(("rx", "ry"), None), P(("rx", "ry"), None, None), P(("rx", "ry"), None)),
        check_vma=False,
    )
```

profile of v0, /device:TPU:0, one launch (start us, length us, event | category | flops | bytes accessed | tf_op | source)
XLA Modules:
  0.0 353.7 jit_solution(7283829084078179492)
XLA Ops:
  0.7 8.8 %fusion.71 = f32[128,1,128]{2,1,0:T(1,128)S(1)} fusion(bf16[128,128,128]{2,1,0:T(8,128)(2,1)} %param.13, f32[128,128,1]{1,2,0:T(1,128)} %bitcast.150), kind=kOutput, calls=%fused_computation.162 | convolution fusion | flops 25165824 | bytes 4325376 | tf_op jit(solution)/shard_map/nij,nj->ni/dot_general | solution.py:29
  15.4 10.5 %all_gather.6 = f32[1024,128]{1,0:T(8,128)S(1)} all-gather(f32[128,128]{1,0:T(8,128)S(1)} %get-tuple-element.7), channel_id=1, replica_groups=mesh['rx'=8,'ry'=4] {'rx'}, dimensions={0}, use_global_device_ids=true | all-gather | bytes 589824 | tf_op jit(solution)/shard_map/all_gather | solution.py:84
  27.5 8.4 %fusion.73 = f32[128,1,128]{2,1,0:T(1,128)S(1)} fusion(f32[128,128,1]{1,2,0:T(1,128)S(1)} %bitcast.162, bf16[128,128,128]{2,1,0:T(8,128)(2,1)} %param.11), kind=kOutput, calls=%fused_computation.164 | convolution fusion | flops 25165824 | bytes 4325376 | tf_op jit(solution)/shard_map/nij,nj->ni/dot_general | solution.py:29
  38.4 5.7 %fusion.35 = bf16[64,128,128]{2,1,0:T(8,128)(2,1)} fusion(bf16[128,128,128]{2,1,0:T(8,128)(2,1)} %param.10, bf16[128,128,128]{2,1,0:T(8,128)(2,1)} %param.14), kind=kOutput, calls=%fused_computation.47 | convolution fusion | flops 538968064 | bytes 8388608 | tf_op jit(solution)/shard_map/nij,njk->nik/dot_general | solution.py:45
  44.1 8.3 %fusion.72 = f32[128,1,128]{2,1,0:T(1,128)S(1)} fusion(f32[128,128,1]{1,2,0:T(1,128)S(1)} %bitcast.149, bf16[128,128,128]{2,1,0:T(8,128)(2,1)} %param.10), kind=kOutput, calls=%fused_computation.163 | convolution fusion | flops 25165824 | bytes 4325376 | tf_op jit(solution)/shard_map/nij,nj->ni/dot_general | solution.py:29
  52.5 8.4 %fusion.6 = f32[128,1,128]{2,1,0:T(1,128)S(1)} fusion(f32[128,128,1]{1,2,0:T(1,128)S(1)} %bitcast.161, bf16[128,2,128,128]{3,2,1,0:T(8,128)(2,1)} %param.12), kind=kOutput, calls=%fused_computation.22 | convolution fusion | flops 25165824 | bytes 4325376 | tf_op jit(solution)/shard_map/nij,nj->ni/dot_general | solution.py:29
  65.5 6.7 %copy.31 = bf16[8,16,128,128]{2,3,1,0:T(8,128)(2,1)} copy(bf16[8,16,128,128]{3,2,1,0:T(8,128)(2,1)} %bitcast.135) | data formatting | bytes 8388608 | tf_op jit(solution)/shard_map/gather | solution.py:59
  75.2 6.5 %copy.35 = bf16[8,16,128,128]{2,3,1,0:T(8,128)(2,1)} copy(bf16[8,16,128,128]{3,2,1,0:T(8,128)(2,1)} %bitcast.136) | data formatting | bytes 8388608 | tf_op jit(solution)/shard_map/gather | solution.py:59
  93.4 6.6 %fusion.74 = f32[128,1,128]{2,1,0:T(1,128)S(1)} fusion(f32[128,128,1]{1,2,0:T(1,128)S(1)} %bitcast.158, bf16[128,128,128]{2,1,0:T(8,128)(2,1)S(1)} %copy-done.5), kind=kOutput, calls=%fused_computation.165 | convolution fusion | flops 25165824 | bytes 4325376 | tf_op jit(solution)/shard_map/nij,nj->ni/dot_general | solution.py:29
  100.0 9.8 %all_gather.7 = f32[1024,128]{1,0:T(8,128)S(1)} all-gather(f32[128,128]{1,0:T(8,128)S(1)} %get-tuple-element.6), channel_id=1, replica_groups=mesh['rx'=8,'ry'=4] {'rx'}, dimensions={0}, use_global_device_ids=true | all-gather | bytes 589824 | tf_op jit(solution)/shard_map/all_gather | solution.py:84
  115.1 8.6 %fusion.4 = f32[128,1,128]{2,1,0:T(1,128)S(1)} fusion(f32[128,128,1]{1,2,0:T(1,128)S(1)} %bitcast.159, bf16[128,2,128,128]{3,2,1,0:T(8,128)(2,1)} %param.12), kind=kOutput, calls=%fused_computation.20 | convolution fusion | flops 25165824 | bytes 4325376 | tf_op jit(solution)/shard_map/nij,nj->ni/dot_general | solution.py:29
  123.7 6.6 %fusion.76 = f32[128,1,128]{2,1,0:T(1,128)S(1)} fusion(f32[128,128,1]{1,2,0:T(1,128)S(1)} %bitcast.160, bf16[128,128,128]{2,1,0:T(8,128)(2,1)S(1)} %copy-done.2), kind=kOutput, calls=%fused_computation.167 | convolution fusion | flops 25165824 | bytes 4325376 | tf_op jit(solution)/shard_map/nij,nj->ni/dot_general | solution.py:29
  130.3 6.6 %fusion.75 = f32[128,1,128]{2,1,0:T(1,128)S(1)} fusion(f32[128,128,1]{1,2,0:T(1,128)S(1)} %bitcast.144, bf16[128,128,128]{2,1,0:T(8,128)(2,1)S(1)} %copy-done.3), kind=kOutput, calls=%fused_computation.166 | convolution fusion | flops 25165824 | bytes 4325376 | tf_op jit(solution)/shard_map/nij,nj->ni/dot_general | solution.py:29
  150.2 8.9 %broadcast_select_fusion.1 = (bf16[8,16,128,128]{2,3,1,0:T(8,128)(2,1)}, bf16[8,16,128,128]{2,3,1,0:T(8,128)(2,1)}, bf16[8,16,128,128]{2,3,1,0:T(8,128)(2,1)}) fusion(bf16[8,16,128,128]{2,3,1,0:T(8,128)(2,1)} %copy.31, pred[8,16]{1,0:T(8,128)(4,1)S(1)} %and_reduce_fusion.1, bf16[8,16,128,128]{2,3,1,0:T(8,128)(2,1)} %copy.35, ...), kind=kLoop, calls=%fused_computation.26 | loop fusion | flops 6291456 | bytes 25165952 | tf_op jit(solution)/shard_map/jit(_where)/select_n | solution.py:61
  159.1 53.8 %all_to_all.25 = bf16[8,16,128,128]{2,3,1,0:T(8,128)(2,1)} all-to-all(bf16[8,16,128,128]{2,3,1,0:T(8,128)(2,1)} %get-tuple-element.11), channel_id=1, replica_groups=mesh['rx'=8,'ry'=4] {'rx'}, dimensions={0} | all-to-all | bytes 8388608 | tf_op jit(solution)/shard_map/all_to_all | solution.py:118
  212.9 52.3 %all_to_all.26 = bf16[8,16,128,128]{2,3,1,0:T(8,128)(2,1)} all-to-all(bf16[8,16,128,128]{2,3,1,0:T(8,128)(2,1)S(1)} %copy-done.4), channel_id=1, replica_groups=mesh['rx'=8,'ry'=4] {'rx'}, dimensions={0} | all-to-all | bytes 8388608 | tf_op jit(solution)/shard_map/all_to_all | solution.py:125
  270.9 6.4 %fusion.26 = f32[64,128,128]{2,1,0:T(8,128)} fusion(bf16[128,128,128]{2,1,0:T(8,128)(2,1)} %param.10, bf16[128,128,128]{2,1,0:T(8,128)(2,1)} %param.14), kind=kOutput, calls=%fused_computation.42 | convolution fusion | flops 537919488 | bytes 10485760 | tf_op jit(solution)/shard_map/nij,njk->nik/dot_general | solution.py:45
  281.4 6.5 %copy.30 = bf16[8,16,128,128]{3,2,1,0:T(8,128)(2,1)} copy(bf16[8,16,128,128]{2,3,1,0:T(8,128)(2,1)} %all_to_all.25) | data formatting | bytes 8388608 | tf_op jit(solution)/shard_map/all_to_all | solution.py:118
  291.0 6.5 %copy.32 = bf16[8,16,128,128]{3,2,1,0:T(8,128)(2,1)} copy(bf16[8,16,128,128]{2,3,1,0:T(8,128)(2,1)} %all_to_all.26) | data formatting | bytes 8388608 | tf_op jit(solution)/shard_map/all_to_all | solution.py:125
  301.8 5.6 %fusion.20 = f32[64,128,128]{2,1,0:T(8,128)} fusion(bf16[64,128,128]{2,1,0:T(8,128)(2,1)S(1)} %gather_fusion.9, bf16[128,128,128]{2,1,0:T(8,128)(2,1)} %param.11, bf16[128,128,128]{2,1,0:T(8,128)(2,1)} %param.14), kind=kOutput, calls=%fused_computation.38 | convolution fusion | flops 537919488 | bytes 10485760 | tf_op jit(solution)/shard_map/nij,njk->nik/dot_general | solution.py:45
  307.4 11.8 %all-to-all-done.3 = bf16[8,16,128,128]{2,3,1,0:T(8,128)(2,1)} async-done(((bf16[8,16,128,128]{2,3,1,0:T(8,128)(2,1)}), bf16[8,16,128,128]{2,3,1,0:T(8,128)(2,1)}, u32[]{:S(2)}, u32[]{:S(2)}) %all-to-all-start.3) | async-done | bytes 4194336 | tf_op jit(solution)/shard_map/all_to_all | solution.py:132
  319.2 6.5 %copy.36 = bf16[8,16,128,128]{3,2,1,0:T(8,128)(2,1)} copy(bf16[8,16,128,128]{2,3,1,0:T(8,128)(2,1)} %all-to-all-done.3) | data formatting | bytes 8388608 | tf_op jit(solution)/shard_map/all_to_all | solution.py:132
  330.0 6.3 %add_convert_fusion = bf16[64,128,128]{2,1,0:T(8,128)(2,1)S(1)} fusion(bf16[64,128,128]{2,1,0:T(8,128)(2,1)} %gather_fusion.13, f32[64,128,128]{2,1,0:T(8,128)} %fusion.26, f32[64,128,128]{2,1,0:T(8,128)} %fusion.20, bf16[64,128,128]{2,1,0:T(8,128)(2,1)} %gather_fusion.11, bf16[128,128,128]{2,1,0:T(8,128)(2,1)} %param.14), kind=kOutput, calls=%fused_computation.24 | convolution fusion | flops 273678336 | bytes 16777216 | tf_op jit(solution)/shard_map/nij,njk->nik/dot_general | solution.py:45
  344.3 4.9 %fusion.47 = f32[64,1,128]{2,1,0:T(1,128)S(1)} fusion(f32[64,128,1]{1,2,0:T(1,128)S(1)} %bitcast.140, bf16[128,128,128]{2,1,0:T(8,128)(2,1)} %param.14), kind=kOutput, calls=%fused_computation.53 | convolution fusion | flops 12582912 | bytes 2162688 | tf_op jit(solution)/shard_map/nij,nj->ni/dot_general | solution.py:29
  (111 shorter events, 81.5 us)
Async XLA Ops:
  0.6 14.0 %copy-start.10 = (s32[64]{0:T(128)S(1)}, s32[64]{0:T(128)}, u32[]{:S(2)}) copy-start(s32[64]{0:T(128)} %param.17) | copy-start | bytes 772
  0.6 14.7 %copy-start.11 = (s32[128,2]{0,1:T(2,128)S(1)}, s32[128,2]{0,1:T(2,128)}, u32[]{:S(2)}) copy-start(s32[128,2]{0,1:T(2,128)} %param.15) | copy-start | bytes 3076
  0.7 25.3 %copy-start.12 = (s32[64]{0:T(128)S(1)}, s32[64]{0:T(128)}, u32[]{:S(2)}) copy-start(s32[64]{0:T(128)} %param.16) | copy-start | bytes 772
  9.5 78.6 %collective-permute-start = (bf16[1,128,128]{2,1,0:T(8,128)(2,1)S(1)}, bf16[1,128,128]{2,1,0:T(8,128)(2,1)S(1)}, u32[]{:S(2)}, u32[]{:S(2)}) collective-permute-start(bf16[1,128,128]{2,1,0:T(8,128)(2,1)S(1)} %get-tuple-element.8), channel_id=1, source_target_pairs={{0,1},{1,2},{2,3},{3,0},{4,5},{5,6},{6,7},{7,4},{8,9},{9,10},{10,1... | collective-permute-start | bytes 98312 | tf_op jit(solution)/shard_map/ppermute | solution.py:20
  12.5 75.5 %collective-permute-start.1 = (bf16[1,128,128]{2,1,0:T(8,128)(2,1)S(1)}, bf16[1,128,128]{2,1,0:T(8,128)(2,1)S(1)}, u32[]{:S(2)}, u32[]{:S(2)}) collective-permute-start(bf16[1,128,128]{2,1,0:T(8,128)(2,1)S(1)} %get-tuple-element.8), channel_id=1, source_target_pairs={{1,0},{2,1},{3,2},{0,3},{5,4},{6,5},{7,6},{4,7},{9,8},{10,9},{11,1... | collective-permute-start | bytes 98312 | tf_op jit(solution)/shard_map/ppermute | solution.py:23
  27.5 8.4 %copy-start = (bf16[128,128,128]{2,1,0:T(8,128)(2,1)S(1)}, bf16[128,128,128]{2,1,0:T(8,128)(2,1)}, u32[]{:S(2)}) copy-start(bf16[128,128,128]{2,1,0:T(8,128)(2,1)} %param.14) | copy-start | bytes 12582916
  52.5 8.5 %copy-start.1 = (bf16[128,128,128]{2,1,0:T(8,128)(2,1)S(1)}, bf16[128,128,128]{2,1,0:T(8,128)(2,1)}, u32[]{:S(2)}) copy-start(bf16[128,128,128]{2,1,0:T(8,128)(2,1)} %param.14) | copy-start | bytes 12582916
  65.5 6.7 %copy-start.6 = (bf16[64,128,128]{2,1,0:T(8,128)(2,1)S(1)}, bf16[64,128,128]{2,1,0:T(8,128)(2,1)}, u32[]{:S(2)}) copy-start(bf16[64,128,128]{2,1,0:T(8,128)(2,1)} %fusion.35) | copy-start | bytes 6291460
  88.0 5.4 %copy-start.8 = (f32[128,128]{1,0:T(8,128)S(1)}, f32[128,128]{1,0:T(8,128)}, u32[]{:S(2)}) copy-start(f32[128,128]{1,0:T(8,128)} %param.9) | copy-start | bytes 196612
  88.8 4.7 %copy-start.5 = (bf16[128,128,128]{2,1,0:T(8,128)(2,1)S(1)}, bf16[128,128,128]{2,1,0:T(8,128)(2,1)}, u32[]{:S(2)}) copy-start(bf16[128,128,128]{2,1,0:T(8,128)(2,1)} %param.13) | copy-start | bytes 12582916
  111.2 12.5 %copy-start.2 = (bf16[128,128,128]{2,1,0:T(8,128)(2,1)S(1)}, bf16[128,128,128]{2,1,0:T(8,128)(2,1)}, u32[]{:S(2)}) copy-start(bf16[128,128,128]{2,1,0:T(8,128)(2,1)} %param.11) | copy-start | bytes 12582916
  111.2 25.7 %collective-permute-start.2 = (bf16[1,128,128]{2,1,0:T(8,128)(2,1)S(1)}, bf16[1,128,128]{2,1,0:T(8,128)(2,1)S(1)}, u32[]{:S(2)}, u32[]{:S(2)}) collective-permute-start(bf16[1,128,128]{2,1,0:T(8,128)(2,1)S(1)} %get-tuple-element.5), channel_id=1, source_target_pairs={{0,1},{1,2},{2,3},{3,0},{4,5},{5,6},{6,7},{7,4},{8,9},{9,10},{10,1... | collective-permute-start | bytes 98312 | tf_op jit(solution)/shard_map/ppermute | solution.py:20
  111.2 25.6 %collective-permute-start.3 = (bf16[1,128,128]{2,1,0:T(8,128)(2,1)S(1)}, bf16[1,128,128]{2,1,0:T(8,128)(2,1)S(1)}, u32[]{:S(2)}, u32[]{:S(2)}) collective-permute-start(bf16[1,128,128]{2,1,0:T(8,128)(2,1)S(1)} %get-tuple-element.5), channel_id=1, source_target_pairs={{1,0},{2,1},{3,2},{0,3},{5,4},{6,5},{7,6},{4,7},{9,8},{10,9},{11,1... | collective-permute-start | bytes 98312 | tf_op jit(solution)/shard_map/ppermute | solution.py:23
  115.1 15.2 %copy-start.3 = (bf16[128,128,128]{2,1,0:T(8,128)(2,1)S(1)}, bf16[128,128,128]{2,1,0:T(8,128)(2,1)}, u32[]{:S(2)}) copy-start(bf16[128,128,128]{2,1,0:T(8,128)(2,1)} %param.10) | copy-start | bytes 12582916
  146.8 12.2 %all-to-all-start = ((bf16[8,16,128]{2,1,0:T(8,128)(2,1)}), bf16[8,16,128]{2,1,0:T(8,128)(2,1)S(1)}, u32[]{:S(2)}, u32[]{:S(2)}) async-start(bf16[8,16,128]{2,1,0:T(8,128)(2,1)} %select_convert_fusion.1), calls=%async_computation | async-start | bytes 65536 | tf_op jit(solution)/shard_map/all_to_all | solution.py:144
  159.1 53.8 %copy-start.4 = (bf16[8,16,128,128]{2,3,1,0:T(8,128)(2,1)S(1)}, bf16[8,16,128,128]{2,3,1,0:T(8,128)(2,1)}, u32[]{:S(2)}) copy-start(bf16[8,16,128,128]{2,3,1,0:T(8,128)(2,1)} %get-tuple-element.9) | copy-start | bytes 12582916
  265.2 54.0 %all-to-all-start.3 = ((bf16[8,16,128,128]{2,3,1,0:T(8,128)(2,1)}), bf16[8,16,128,128]{2,3,1,0:T(8,128)(2,1)}, u32[]{:S(2)}, u32[]{:S(2)}) async-start(bf16[8,16,128,128]{2,3,1,0:T(8,128)(2,1)} %get-tuple-element.10), calls=%async_computation.3 | async-start | bytes 8388608 | tf_op jit(solution)/shard_map/all_to_all | solution.py:132
  281.3 58.3 %copy-start.9 = (f32[64,128]{1,0:T(8,128)}, f32[64,128]{1,0:T(8,128)S(1)}, u32[]{:S(2)}) copy-start(f32[64,128]{1,0:T(8,128)S(1)} %get-tuple-element.4) | copy-start | bytes 98308
  336.3 17.2 %copy-start.7 = (bf16[64,128,128]{2,1,0:T(8,128)(2,1)}, bf16[64,128,128]{2,1,0:T(8,128)(2,1)S(1)}, u32[]{:S(2)}) copy-start(bf16[64,128,128]{2,1,0:T(8,128)(2,1)S(1)} %add_convert_fusion) | copy-start | bytes 6291460
  341.0 8.3 %all-to-all-start.4 = ((bf16[8,16,128]{2,1,0:T(8,128)(2,1)}), bf16[8,16,128]{2,1,0:T(8,128)(2,1)S(1)}, u32[]{:S(2)}, u32[]{:S(2)}) async-start(bf16[8,16,128]{2,1,0:T(8,128)(2,1)} %select_convert_fusion), calls=%async_computation.4 | async-start | bytes 65536 | tf_op jit(solution)/shard_map/all_to_all | solution.py:163
where the time goes:
time: 358 us; the launch traced here: 354 us
  blocking collectives  127 us (35%)
  matrix products  115 us (32%)
  local copies, waits for them, and re-layouts  66.1 us (18%)
  starting transfers between devices  20.5 us (6%)
  other arithmetic  12 us (3%)
  waiting for transfers between devices  11.8 us (3%)
    dot_general x13, matrix products, mat_vec(): jnp.einsum('nij,nj->ni', matrix.astype(jnp.float32), vector, precision=la...  82.3 us
    all_to_all x1, blocking collectives, body(): lax.all_to_all(pack_slots(odd_prol, send_items, send_filled, line_size, c...  53.8 us
    all_to_all x1, blocking collectives, body(): lax.all_to_all(pack_slots(behind, send_items, send_filled, line_size, cap...  52.3 us
    dot_general x4, matrix products, plain_product(): jnp.einsum('nij,njk->nik', left_mat, right_mat, preferred_element_type=jn...  23.9 us
    gather x7, local copies, waits for them, and re-layouts, pack_slots(): taken = values[chosen]  23.5 us
    all_gather x2, blocking collectives, operate(): whole_line = lax.all_gather(vector, 'rx', axis=0, tiled=True)  20.4 us
    gather x4, local copies, waits for them, and re-layouts, unpack(): received.reshape((line_size * capacity,) + received.shape[2:])[recv_slot]  12.4 us
    all_to_all x1, waiting for transfers between devices, body(): lax.all_to_all(pack_slots(inner, send_items, send_filled, line_size, capa...  11.8 us
  transfers between devices with their start and end apart: 7, of which 1 were waited for; matrix products, arithmetic and copies ran while one was open for 38% of the time, Pallas kernels for 0%

commit v1 on v0

v1 whole, which is shorter than its diff:
```python
import functools

import jax
import jax.numpy as jnp
from jax import lax
from jax.experimental import pallas as pl
from jax.experimental.pallas import tpu as pltpu
from jax.sharding import PartitionSpec as P

OMEGA = 0.7
THETA = 0.08
MESH = pl.DeviceIdType.MESH
BF = jnp.bfloat16
F32 = jnp.float32

NT = (((1,), (1,)), ((), ()))
NN = (((1,), (0,)), ((), ()))
TN = (((0,), (0,)), ((), ()))


def dot(left, right, dims):
    return lax.dot_general(left, right, dims, preferred_element_type=F32)


def two_parts(values):
    high = values.astype(BF)
    low = (values - high.astype(F32)).astype(BF)
    return jnp.concatenate([high, low], axis=0)


def kernel(
    n,
    m,
    cap,
    rows,
    idx,
    rhs,
    h_diag,
    h_pair,
    h_far,
    h_inv,
    h_prol,
    fine_out,
    h_blocks,
    rest_out,
    v_diag,
    v_pair,
    v_far,
    v_inv,
    v_prol,
    out_blocks,
    send_p,
    send_b,
    send_i,
    recv_p,
    recv_b,
    recv_i,
    pre,
    it_send,
    it_recv,
    side_recv,
    line_vals,
    side_vals,
    mate_rows,
    far_rows,
    side_rows,
    iterate,
    defect,
    restr,
    corr,
    odd_corr,
    piece_send,
    piece_recv,
    back_send,
    back_recv,
    load_sems,
    s_sems,
    r_sems,
    ss_sems,
    sr_sems,
):
    half = rows // 2
    slots = (n - 1) * cap
    mate_at, far_at, side_at = 0, rows, 2 * rows
    recv_at = 3 * rows
    send_at = recv_at + half
    item_at = send_at + half
    back_at = item_at + slots
    line = lax.axis_index("rx")
    col = lax.axis_index("ry")
    peers = [lax.rem(line + o, n) for o in range(1, n)]
    back_peers = [lax.rem(line + n - o, n) for o in range(1, n)]
    below, above = lax.rem(col + m - 1, m), lax.rem(col + 1, m)

    loads = [
        pltpu.make_async_copy(src, dst, load_sems.at[i])
        for i, (src, dst) in enumerate(
            [(h_inv, v_inv), (h_prol, v_prol), (h_diag, v_diag), (h_pair, v_pair), (h_far, v_far)]
        )
    ]
    for load in loads:
        load.start()

    barrier = pltpu.get_barrier_semaphore()
    for peer in peers:
        pl.semaphore_signal(barrier, inc=1, device_id=(peer, col), device_id_type=MESH)
    for side in (below, above):
        pl.semaphore_signal(barrier, inc=1, device_id=(line, side), device_id_type=MESH)
    pl.semaphore_wait(barrier, n + 1)

    def to_peer(kind, o, src, dst, back=False):
        return pltpu.make_async_remote_copy(
            src_ref=src,
            dst_ref=dst,
            send_sem=s_sems.at[kind, o],
            recv_sem=r_sems.at[kind, o],
            device_id=((back_peers if back else peers)[o], col),
            device_id_type=MESH,
        )

    def iterate_copies(turn):
        copies = [
            to_peer(turn, o, it_send.at[turn], it_recv.at[turn, o]) for o in range(n - 1)
        ]
        for k, side in enumerate((above, below)):
            copies.append(
                pltpu.make_async_remote_copy(
                    src_ref=it_send.at[turn],
                    dst_ref=side_recv.at[turn, k],
                    send_sem=ss_sems.at[turn, k],
                    recv_sem=sr_sems.at[turn, k],
                    device_id=(line, side),
                    device_id_type=MESH,
                )
            )
        return copies

    row_id = lax.broadcasted_iota(jnp.int32, (8, 128), 0)

    def groups(count, body):
        def step(g, carry):
            body(pl.multiple_of(g * 8, 8))
            return carry

        lax.fori_loop(0, count // 8, step, 0)

    def exact_rows(values, first, matrix, dims):
        both = two_parts(values)
        total = jnp.zeros((8, 128), F32)
        for r in range(8):
            part = dot(both, matrix(first + r), dims)
            total = jnp.where(row_id == r, part[:8] + part[8:], total)
        return total

    def gather_rows(turn):
        line_vals[0] = it_send[turn].astype(F32)
        for o in range(n - 1):
            line_vals[o + 1] = it_recv[turn, o].astype(F32)
        side_vals[...] = side_recv[turn].astype(F32)

        def step(g, carry):
            for r in range(8):
                i = g * 8 + r
                a = idx[mate_at + i]
                b = idx[far_at + i]
                c = idx[side_at + i]
                mate_rows[pl.ds(i, 1), :] = line_vals[a // rows, pl.ds(a % rows, 1), :]
                far_rows[pl.ds(i, 1), :] = line_vals[b // rows, pl.ds(b % rows, 1), :]
                side_rows[pl.ds(i, 1), :] = side_vals[c // rows, pl.ds(c % rows, 1), :]
            return carry

        lax.fori_loop(0, rows // 8, step, 0)

    def subtract_operator():
        def body(first):
            at = pl.ds(first, 8)
            own = two_parts(iterate[at, :])
            mates = mate_rows[at, :].astype(BF)
            fars = far_rows[at, :].astype(BF)
            sides = side_rows[at, :].astype(BF)
            total = jnp.zeros((8, 128), F32)
            for r in range(8):
                i = first + r
                main = dot(own, v_diag[i], NT)
                part = main[:8] + main[8:] + dot(mates, v_pair[i], NT)
                part = part + dot(fars, v_far[i, 0], NT) + dot(sides, v_far[i, 1], NT)
                total = jnp.where(row_id == r, part, total)
            defect[at, :] = rhs[at, :] - total

        groups(rows, body)

    loads[0].wait()

    def first_sweep(first):
        at = pl.ds(first, 8)
        iterate[at, :] = OMEGA * exact_rows(rhs[at, :], first, lambda i: v_inv[i], NT)

    groups(rows, first_sweep)
    it_send[0] = iterate[...].astype(BF)
    it_copies = iterate_copies(0)
    for copy in it_copies:
        copy.start()

    loads[1].wait()
    p_copies = []
    for o in range(n - 1):

        def pack(k, carry):
            send_p[o, k] = v_prol[2 * idx[item_at + o * cap + k] + 1]
            return carry

        lax.fori_loop(0, cap, pack, 0)
        p_copies.append(to_peer(2, o, send_p.at[o], recv_p.at[o]))
        p_copies[-1].start()

    for load in loads[2:]:
        load.wait()
    for copy in it_copies:
        copy.wait()
    gather_rows(0)
    subtract_operator()

    def second_sweep(first):
        at = pl.ds(first, 8)
        step = exact_rows(defect[at, :], first, lambda i: v_inv[i], NT)
        iterate[at, :] = iterate[at, :] + OMEGA * step

    groups(rows, second_sweep)
    it_send[1] = iterate[...].astype(BF)
    it_copies = iterate_copies(1)
    for copy in it_copies:
        copy.start()

    b_copies = []
    for o in range(n - 1):

        def behind(k, carry):
            i = 2 * idx[item_at + o * cap + k] + 1
            send_b[o, k] = dot(v_prol[i], v_pair[i], TN).astype(BF)
            return carry

        lax.fori_loop(0, cap, behind, 0)
        b_copies.append(to_peer(3, o, send_b.at[o], recv_b.at[o]))
        b_copies[-1].start()

    i_copies = []
    for o in range(n - 1):

        def inner(k, carry):
            i = 2 * idx[item_at + o * cap + k] + 1
            block = v_prol[i]
            lower = dot(block, v_diag[i], TN).astype(BF)
            send_i[o, k] = dot(lower, block, NN).astype(BF)
            return carry

        lax.fori_loop(0, cap, inner, 0)
        i_copies.append(to_peer(4, o, send_i.at[o], recv_i.at[o]))

    for copy in it_copies:
        copy.wait()
    gather_rows(1)
    subtract_operator()

    def restrict(first):
        at = pl.ds(first, 8)
        mate_rows[at, :] = exact_rows(defect[at, :], first, lambda i: v_prol[i], NN)

    groups(rows, restrict)
    piece_copies = []
    for o in range(n - 1):
        for k in range(cap):
            i = 2 * idx[item_at + o * cap + k] + 1
            piece_send[o, pl.ds(k, 1), :] = mate_rows[pl.ds(i, 1), :]
        piece_copies.append(to_peer(5, o, piece_send.at[o], piece_recv.at[o]))
        piece_copies[-1].start()
    for copy in i_copies:
        copy.start()

    for copy in p_copies:
        copy.wait()
    for copy in b_copies:
        copy.wait()

    def products(c, carry):
        slot = idx[recv_at + c]
        block = v_prol[2 * c]
        upper = dot(block, v_diag[2 * c], TN).astype(BF)
        across = dot(block, v_pair[2 * c], TN).astype(BF)
        total = dot(upper, block, NN)
        total = total + dot(across, recv_p[slot // cap, slot % cap], NN)
        pre[c] = total + dot(recv_b[slot // cap, slot % cap], block, NN)
        return carry

    lax.fori_loop(0, half, products, 0)

    for copy in piece_copies:
        copy.wait()

    def restricted(g, carry):
        for r in range(8):
            c = g * 8 + r
            slot = idx[recv_at + c]
            piece = piece_recv[slot // cap, pl.ds(slot % cap, 1), :]
            restr[pl.ds(c, 1), :] = mate_rows[pl.ds(2 * c, 1), :] + piece
        return carry

    lax.fori_loop(0, half // 8, restricted, 0)
    rest_out[...] = restr[...]

    for copy in i_copies:
        copy.wait()

    def finish(c, carry):
        slot = idx[recv_at + c]
        last = recv_i[slot // cap, slot % cap].astype(F32)
        out_blocks[c] = (pre[c] + last).astype(BF)
        return carry

    lax.fori_loop(0, half, finish, 0)
    store = pltpu.make_async_copy(out_blocks, h_blocks, load_sems.at[5])
    store.start()

    def correct(first):
        at = pl.ds(first, 8)
        value = restr[at, :]
        start = THETA * value
        moved = exact_rows(start, first, lambda c: out_blocks[c], NT)
        corr[at, :] = start + THETA * (value - moved)

    groups(half, correct)
    back_copies = []
    for o in range(n - 1):
        for k in range(cap):
            c = idx[back_at + o * cap + k]
            back_send[o, pl.ds(k, 1), :] = corr[pl.ds(c, 1), :]
        back_copies.append(to_peer(6, o, back_send.at[o], back_recv.at[o], back=True))
        back_copies[-1].start()

    def lift_even(first):
        at = pl.ds(first, 8)
        odd_corr[at, :] = exact_rows(corr[at, :], first, lambda c: v_prol[2 * c], NT)
        for r in range(8):
            i = 2 * (first + r)
            fine_out[pl.ds(i, 1), :] = iterate[pl.ds(i, 1), :] + odd_corr[pl.ds(first + r, 1), :]

    groups(half, lift_even)
    for copy in back_copies:
        copy.wait()

    def take_back(g, carry):
        for r in range(8):
            j = g * 8 + r
            slot = idx[send_at + j]
            odd_corr[pl.ds(j, 1), :] = back_recv[slot // cap, pl.ds(slot % cap, 1), :]
        return carry

    lax.fori_loop(0, half // 8, take_back, 0)

    def lift_odd(first):
        at = pl.ds(first, 8)
        corr[at, :] = exact_rows(odd_corr[at, :], first, lambda j: v_prol[2 * j + 1], NT)
        for r in range(8):
            i = 2 * (first + r) + 1
            fine_out[pl.ds(i, 1), :] = iterate[pl.ds(i, 1), :] + corr[pl.ds(first + r, 1), :]

    groups(half, lift_odd)
    store.wait()


def tables(n, m, cap, rows, col_index, partner, odd_owner):
    half = rows // 2
    slots = (n - 1) * cap
    line = lax.axis_index("rx")
    col = lax.axis_index("ry")
    mate = jnp.stack([partner, 2 * odd_owner], axis=1).reshape(rows)

    def line_slot(row):
        return (line - row // rows // m) % n * rows + row % rows

    below = (col_index[:, 1] // rows) % m == (col - 1) % m
    side = jnp.where(below, 0, rows) + col_index[:, 1] % rows
    order = jnp.arange(half, dtype=jnp.int32)

    def slot_of(offset, key):
        same = offset[:, None] == offset[None, :]
        rank = jnp.sum(same & (key[None, :] < key[:, None]), axis=1, dtype=jnp.int32)
        return (offset - 1) * cap + rank

    send = slot_of((odd_owner // half // m - line) % n, odd_owner)
    recv = slot_of((line - partner // rows // m) % n, order)

    def inverse(slot):
        hits = slot[None, :] == jnp.arange(slots, dtype=jnp.int32)[:, None]
        return jnp.sum(jnp.where(hits, order[None, :], 0), axis=1, dtype=jnp.int32)

    return jnp.concatenate(
        [line_slot(mate), line_slot(col_index[:, 0]), side, recv, send, inverse(send), inverse(recv)]
    )


def body(n, m, rhs, a_diag, a_pair, a_far, approx_inv, prolong, col_index, partner, odd_owner):
    rows, width = rhs.shape
    half = rows // 2
    cap = half // (n // 2)
    idx = tables(n, m, cap, rows, col_index, partner, odd_owner)
    vmem = pl.BlockSpec(memory_space=pltpu.VMEM)
    hbm = pl.BlockSpec(memory_space=pl.ANY)
    block = (width, width)
    slot_blocks = pltpu.VMEM((n - 1, cap) + block, BF)
    row_vals = pltpu.VMEM((rows, width), F32)
    half_vals = pltpu.VMEM((half, width), F32)
    slot_vals = pltpu.VMEM((n - 1, cap, width), F32)
    row_blocks = pltpu.VMEM((rows,) + block, BF)
    dma = pltpu.SemaphoreType.DMA
    fine, blocks, restricted = pl.pallas_call(
        functools.partial(kernel, n, m, cap, rows),
        out_shape=(
            jax.ShapeDtypeStruct((rows, width), F32),
            jax.ShapeDtypeStruct((half,) + block, BF),
            jax.ShapeDtypeStruct((half, width), F32),
        ),
        in_specs=[pl.BlockSpec(memory_space=pltpu.SMEM), vmem] + [hbm] * 5,
        out_specs=(vmem, hbm, vmem),
        scratch_shapes=[
            row_blocks,
            row_blocks,
            pltpu.VMEM((rows, 2) + block, BF),
            row_blocks,
            row_blocks,
            pltpu.VMEM((half,) + block, BF),
            slot_blocks,
            slot_blocks,
            slot_blocks,
            slot_blocks,
            slot_blocks,
            slot_blocks,
            pltpu.VMEM((half,) + block, F32),
            pltpu.VMEM((2, rows, width), BF),
            pltpu.VMEM((2, n - 1, rows, width), BF),
            pltpu.VMEM((2, 2, rows, width), BF),
            pltpu.VMEM((n, rows, width), F32),
            pltpu.VMEM((2, rows, width), F32),
            row_vals,
            row_vals,
            row_vals,
            row_vals,
            row_vals,
            half_vals,
            half_vals,
            half_vals,
            slot_vals,
            slot_vals,
            slot_vals,
            slot_vals,
            dma((6,)),
            dma((7, n - 1)),
            dma((7, n - 1)),
            dma((2, 2)),
            dma((2, 2)),
        ],
        compiler_params=pltpu.CompilerParams(
            collective_id=0, has_side_effects=True, vmem_limit_bytes=61 * 1024 * 1024
        ),
    )(idx, rhs, a_diag, a_pair, a_far, approx_inv, prolong)
    return (fine, blocks, restricted)


def solution(mesh):
    n, m = mesh.shape["rx"], mesh.shape["ry"]
    return jax.shard_map(
        functools.partial(body, n, m),
        mesh=mesh,
        in_specs=(
            P(("rx", "ry"), None),
            P(("rx", "ry"), None, None),
            P(("rx", "ry"), None, None),
            P(("rx", "ry"), None, None, None),
            P(("rx", "ry"), None, None),
            P(("rx", "ry"), None, None),
            P(("rx", "ry"), None),
            P(("rx", "ry")),
            P(("rx", "ry")),
        ),
        out_specs=(P(("rx", "ry"), None), P(("rx", "ry"), None, None), P(("rx", "ry"), None)),
        check_vma=False,
    )
```

time: 358 us -> 174 us (0.49); the launches traced: 354 us -> 174 us
  Pallas kernels: 0 us -> 163 us
  blocking collectives: 127 us -> 0 us
  matrix products: 115 us -> 0 us
  local copies, waits for them, and re-layouts: 66.1 us -> 6.16 us
  starting transfers between devices: 20.5 us -> 0 us
  waiting for transfers between devices: 11.8 us -> 0 us
  other arithmetic: 12 us -> 3.47 us
    pallas_call x0 -> x1, Pallas kernels: none -> 163 us  [body(): pl.pallas_call(functools.partial(kernel, n, m, cap, rows), out_shape=(jax...]
    dot_general x20 -> x0, matrix products: 115 us -> none  [the longest x13 82.3 us: mat_vec(): jnp.einsum('nij,nj->ni', matrix.astype(jnp.float32), vector, precision=la...]
    all_to_all x2 -> x0, blocking collectives: 106 us -> none  [the longest x1 53.8 us: body(): lax.all_to_all(pack_slots(odd_prol, send_items, send_filled, line_size, c...]
    gather x18 -> x0, local copies, waits for them, and re-layouts: 40.6 us -> none  [the longest x7 23.5 us: pack_slots(): taken = values[chosen]]
    all_gather x2 -> x0, blocking collectives: 20.4 us -> none  [operate(): whole_line = lax.all_gather(vector, 'rx', axis=0, tiled=True)]
    all_to_all x3 -> x0, local copies, waits for them, and re-layouts: 19.4 us -> none  [the longest x1 6.52 us: body(): lax.all_to_all(pack_slots(odd_prol, send_items, send_filled, line_size, c...]
    all_to_all x3 -> x0, waiting for transfers between devices: 11.8 us -> none  [the longest x1 11.8 us: body(): lax.all_to_all(pack_slots(inner, send_items, send_filled, line_size, capa...]
    all_to_all x3 -> x0, starting transfers between devices: 11.5 us -> none  [the longest x1 4.83 us: body(): lax.all_to_all(pack_slots(inner, send_items, send_filled, line_size, capa...]
  transfers between devices with their start and end apart: 7 -> 0, of which waited for: 1 -> 0; matrix products, arithmetic and copies ran while one was open for 38% -> 0% of each run, Pallas kernels for 0% -> 0%
where the time goes in v1:
time: 174 us
  Pallas kernels  163 us (94%)
  local copies, waits for them, and re-layouts  6.16 us (4%)
  other arithmetic  3.47 us (2%)
    pallas_call x1, Pallas kernels, body(): pl.pallas_call(functools.partial(kernel, n, m, cap, rows), out_shape=(jax...  163 us
    unnamed x5, local copies, waits for them, and re-layouts  5.26 us

profile of v1, /device:TPU:0, one launch (start us, length us, event | category | flops | bytes accessed | tf_op | source)
XLA Modules:
  0.0 173.7 jit_solution(1660593208788250549)
XLA Ops:
  0.7 0.8 fusion.3
  1.4 0.7 and_select_fusion
  2.1 0.7 pad_add_fusion
  2.8 0.9 convert_reduce_fusion
  3.7 0.1 select_reduce_fusion.1
  3.8 0.2 convert_reduce_fusion.1
  4.0 0.1 select_reduce_fusion
  4.1 0.1 copy.14
  4.2 0.1 reshape.17
  4.4 0.7 concatenate.3.idx
  5.1 163.3 %shard_map.112 = (f32[128,128]{1,0:T(8,128)}, bf16[64,128,128]{2,1,0:T(8,128)(2,1)}, f32[64,128]{1,0:T(8,128)}) custom-call(s32[736]{0:T(1024)} %concatenate.3.idx, f32[128,128]{1,0:T(8,128)} %rhs.1, bf16[128,128,128]{2,1,0:T(8,128)(2,1)} %h_diag.1, bf16[128,128,128]{2,1,0:T(8,128)(2,1)} %h_pair.1, bf16[128,2,128,128]{3,2,1,0:T(8,128)(2,1)} %h_far.1, ...), custom_call_target="tpu_custom_call" | custom-call | tf_op jit(solution)/shard_map/pallas_call | solution.py:415
  168.4 0.0 copy-start
  168.4 1.5 copy.18
  169.9 3.2 %copy.19 = bf16[64,128,128]{2,1,0:T(8,128)(2,1)} copy(bf16[64,128,128]{2,1,0:T(8,128)(2,1)} %get-tuple-element.12) | data formatting | bytes 4194304
  173.0 0.0 copy-done
  173.0 0.6 copy.20
  (3 shorter events, 0.0 us)
Async XLA Ops:
  168.4 4.6 %copy-start = (f32[64,128]{1,0:T(8,128)S(1)}, f32[64,128]{1,0:T(8,128)}, u32[]{:S(2)}) copy-start(f32[64,128]{1,0:T(8,128)} %get-tuple-element.13) | copy-start | bytes 98308

commit v2 on v1

--- a/solution.py
+++ b/solution.py
@@ -95,7 +95,7 @@
     loads = [
         pltpu.make_async_copy(src, dst, load_sems.at[i])
         for i, (src, dst) in enumerate(
-            [(h_inv, v_inv), (h_prol, v_prol), (h_diag, v_diag), (h_pair, v_pair), (h_far, v_far)]
+            [(h_prol, v_prol), (h_inv, v_inv), (h_pair, v_pair), (h_diag, v_diag), (h_far, v_far)]
         )
     ]
     for load in loads:
@@ -106,8 +106,6 @@
         pl.semaphore_signal(barrier, inc=1, device_id=(peer, col), device_id_type=MESH)
     for side in (below, above):
         pl.semaphore_signal(barrier, inc=1, device_id=(line, side), device_id_type=MESH)
-    pl.semaphore_wait(barrier, n + 1)
-
     def to_peer(kind, o, src, dst, back=False):
         return pltpu.make_async_remote_copy(
             src_ref=src,
@@ -190,6 +188,20 @@
         groups(rows, body)
 
     loads[0].wait()
+    for o in range(n - 1):
+
+        def pack(k, carry):
+            for r in range(4):
+                send_p[o, 4 * k + r] = v_prol[2 * idx[item_at + o * cap + 4 * k + r] + 1]
+            return carry
+
+        lax.fori_loop(0, cap // 4, pack, 0)
+    pl.semaphore_wait(barrier, n + 1)
+    p_copies = [to_peer(2, o, send_p.at[o], recv_p.at[o]) for o in range(n - 1)]
+    for copy in p_copies:
+        copy.start()
+
+    loads[1].wait()
 
     def first_sweep(first):
         at = pl.ds(first, 8)
@@ -201,19 +213,21 @@
     for copy in it_copies:
         copy.start()
 
-    loads[1].wait()
-    p_copies = []
+    loads[2].wait()
+    b_copies = []
     for o in range(n - 1):
 
-        def pack(k, carry):
-            send_p[o, k] = v_prol[2 * idx[item_at + o * cap + k] + 1]
+        def behind(k, carry):
+            for r in range(4):
+                i = 2 * idx[item_at + o * cap + 4 * k + r] + 1
+                send_b[o, 4 * k + r] = dot(v_prol[i], v_pair[i], TN).astype(BF)
             return carry
 
-        lax.fori_loop(0, cap, pack, 0)
-        p_copies.append(to_peer(2, o, send_p.at[o], recv_p.at[o]))
-        p_copies[-1].start()
-
-    for load in loads[2:]:
+        lax.fori_loop(0, cap // 4, behind, 0)
+        b_copies.append(to_peer(3, o, send_b.at[o], recv_b.at[o]))
+        b_copies[-1].start()
+
+    for load in loads[3:]:
         load.wait()
     for copy in it_copies:
         copy.wait()
@@ -231,30 +245,20 @@
     for copy in it_copies:
         copy.start()
 
-    b_copies = []
-    for o in range(n - 1):
-
-        def behind(k, carry):
-            i = 2 * idx[item_at + o * cap + k] + 1
-            send_b[o, k] = dot(v_prol[i], v_pair[i], TN).astype(BF)
-            return carry
-
-        lax.fori_loop(0, cap, behind, 0)
-        b_copies.append(to_peer(3, o, send_b.at[o], recv_b.at[o]))
-        b_copies[-1].start()
-
     i_copies = []
     for o in range(n - 1):
 
         def inner(k, carry):
-            i = 2 * idx[item_at + o * cap + k] + 1
-            block = v_prol[i]
-            lower = dot(block, v_diag[i], TN).astype(BF)
-            send_i[o, k] = dot(lower, block, NN).astype(BF)
+            for r in range(4):
+                i = 2 * idx[item_at + o * cap + 4 * k + r] + 1
+                block = v_prol[i]
+                lower = dot(block, v_diag[i], TN).astype(BF)
+                send_i[o, 4 * k + r] = dot(lower, block, NN).astype(BF)
             return carry
 
-        lax.fori_loop(0, cap, inner, 0)
+        lax.fori_loop(0, cap // 4, inner, 0)
         i_copies.append(to_peer(4, o, send_i.at[o], recv_i.at[o]))
+        i_copies[-1].start()
 
     for copy in it_copies:
         copy.wait()
@@ -273,25 +277,25 @@
             piece_send[o, pl.ds(k, 1), :] = mate_rows[pl.ds(i, 1), :]
         piece_copies.append(to_peer(5, o, piece_send.at[o], piece_recv.at[o]))
         piece_copies[-1].start()
-    for copy in i_copies:
-        copy.start()
 
     for copy in p_copies:
         copy.wait()
     for copy in b_copies:
         copy.wait()
 
-    def products(c, carry):
-        slot = idx[recv_at + c]
-        block = v_prol[2 * c]
-        upper = dot(block, v_diag[2 * c], TN).astype(BF)
-        across = dot(block, v_pair[2 * c], TN).astype(BF)
-        total = dot(upper, block, NN)
-        total = total + dot(across, recv_p[slot // cap, slot % cap], NN)
-        pre[c] = total + dot(recv_b[slot // cap, slot % cap], block, NN)
+    def products(g, carry):
+        for r in range(4):
+            c = 4 * g + r
+            slot = idx[recv_at + c]
+            block = v_prol[2 * c]
+            upper = dot(block, v_diag[2 * c], TN).astype(BF)
+            across = dot(block, v_pair[2 * c], TN).astype(BF)
+            total = dot(upper, block, NN)
+            total = total + dot(across, recv_p[slot // cap, slot % cap], NN)
+            pre[c] = total + dot(recv_b[slot // cap, slot % cap], block, NN)
         return carry
 
-    lax.fori_loop(0, half, products, 0)
+    lax.fori_loop(0, half // 4, products, 0)
 
     for copy in piece_copies:
         copy.wait()
@@ -310,24 +314,24 @@
     for copy in i_copies:
         copy.wait()
 
-    def finish(c, carry):
-        slot = idx[recv_at + c]
-        last = recv_i[slot // cap, slot % cap].astype(F32)
-        out_blocks[c] = (pre[c] + last).astype(BF)
-        return carry
-
-    lax.fori_loop(0, half, finish, 0)
-    store = pltpu.make_async_copy(out_blocks, h_blocks, load_sems.at[5])
-    store.start()
-
-    def correct(first):
+    def finish(first):
         at = pl.ds(first, 8)
         value = restr[at, :]
         start = THETA * value
-        moved = exact_rows(start, first, lambda c: out_blocks[c], NT)
+        both = two_parts(start)
+        moved = jnp.zeros((8, 128), F32)
+        for r in range(8):
+            slot = idx[recv_at + first + r]
+            last = recv_i[slot // cap, slot % cap].astype(F32)
+            made = (pre[first + r] + last).astype(BF)
+            out_blocks[first + r] = made
+            part = dot(both, made, NT)
+            moved = jnp.where(row_id == r, part[:8] + part[8:], moved)
         corr[at, :] = start + THETA * (value - moved)
 
-    groups(half, correct)
+    groups(half, finish)
+    store = pltpu.make_async_copy(out_blocks, h_blocks, load_sems.at[5])
+    store.start()
     back_copies = []
     for o in range(n - 1):
         for k in range(cap):
@@ -365,6 +369,23 @@
 
     groups(half, lift_odd)
     store.wait()
+
+
+def hand_over(fine, blocks, rest, fine_out, blocks_out, rest_out, sems):
+    count = sems.shape[0] - 2
+    size = blocks.shape[0] // count
+    copies = [
+        pltpu.make_async_copy(
+            blocks.at[pl.ds(k * size, size)], blocks_out.at[pl.ds(k * size, size)], sems.at[k]
+        )
+        for k in range(count)
+    ]
+    copies.append(pltpu.make_async_copy(fine, fine_out, sems.at[count]))
+    copies.append(pltpu.make_async_copy(rest, rest_out, sems.at[count + 1]))
+    for copy in copies:
+        copy.start()
+    for copy in copies:
+        copy.wait()
 
 
 def tables(n, m, cap, rows, col_index, partner, odd_owner):
@@ -462,7 +483,13 @@
             collective_id=0, has_side_effects=True, vmem_limit_bytes=61 * 1024 * 1024
         ),
     )(idx, rhs, a_diag, a_pair, a_far, approx_inv, prolong)
-    return (fine, blocks, restricted)
+    return pl.pallas_call(
+        hand_over,
+        out_shape=[jax.ShapeDtypeStruct(a.shape, a.dtype) for a in (fine, blocks, restricted)],
+        in_specs=[hbm] * 3,
+        out_specs=[hbm] * 3,
+        scratch_shapes=[dma((10,))],
+    )(fine, blocks, restricted)
 
 
 def solution(mesh):

time: 174 us -> 233 us (1.34)
  Pallas kernels: 163 us -> 227 us
  local copies, waits for them, and re-layouts: 6.16 us -> 0.91 us
    pallas_call x0 -> x1, Pallas kernels: none -> 67.7 us  [body(): pl.pallas_call(hand_over, out_shape=[jax.ShapeDtypeStruct(a.shape, a.dtyp...]
    unnamed x5 -> x0, local copies, waits for them, and re-layouts: 5.26 us -> none
    pallas_call x1, Pallas kernels: 163 us -> 159 us  [body(): pl.pallas_call(functools.partial(kernel, n, m, cap, rows), out_shape=(jax...]
where the time goes in v2:
time: 233 us; the launch traced here: 232 us
  Pallas kernels  227 us (97%)
  other arithmetic  3.47 us (1%)
    pallas_call x1, Pallas kernels, body(): pl.pallas_call(functools.partial(kernel, n, m, cap, rows), out_shape=(jax...  159 us
    pallas_call x1, Pallas kernels, body(): pl.pallas_call(hand_over, out_shape=[jax.ShapeDtypeStruct(a.shape, a.dtyp...  67.7 us

profile of v2, /device:TPU:0, one launch (start us, length us, event | category | flops | bytes accessed | tf_op | source)
XLA Modules:
  0.0 232.1 jit_solution(10357489060464841990)
XLA Ops:
  0.7 0.8 fusion.3
  1.4 0.7 and_select_fusion
  2.1 0.7 pad_add_fusion
  2.8 0.9 convert_reduce_fusion
  3.7 0.1 select_reduce_fusion.1
  3.8 0.2 convert_reduce_fusion.1
  4.0 0.1 select_reduce_fusion
  4.1 0.1 copy.14
  4.2 0.1 reshape.17
  4.4 0.7 concatenate.3.idx
  5.1 159.3 %shard_map.112 = (f32[128,128]{1,0:T(8,128)}, bf16[64,128,128]{2,1,0:T(8,128)(2,1)}, f32[64,128]{1,0:T(8,128)}) custom-call(s32[736]{0:T(1024)} %concatenate.3.idx, f32[128,128]{1,0:T(8,128)} %rhs.1, bf16[128,128,128]{2,1,0:T(8,128)(2,1)} %h_diag.1, bf16[128,128,128]{2,1,0:T(8,128)(2,1)} %h_pair.1, bf16[128,2,128,128]{3,2,1,0:T(8,128)(2,1)} %h_far.1, ...), custom_call_target="tpu_custom_call" | custom-call | tf_op jit(solution)/shard_map/pallas_call | solution.py:436
  164.4 67.7 %shard_map.113 = (f32[128,128]{1,0:T(8,128)}, bf16[64,128,128]{2,1,0:T(8,128)(2,1)}, f32[64,128]{1,0:T(8,128)}) custom-call(f32[128,128]{1,0:T(8,128)} %get-tuple-element.6.fine, bf16[64,128,128]{2,1,0:T(8,128)(2,1)} %get-tuple-element.7.blocks, f32[64,128]{1,0:T(8,128)} %get-tuple-element.8.rest), custom_call_target="tpu_custom_call" | custom-call | tf_op jit(solution)/shard_map/pallas_call | solution.py:486
  (3 shorter events, 0.0 us)

commit v3 on v2

--- a/solution.py
+++ b/solution.py
@@ -116,10 +116,26 @@
             device_id_type=MESH,
         )
 
-    def iterate_copies(turn):
-        copies = [
-            to_peer(turn, o, it_send.at[turn], it_recv.at[turn, o]) for o in range(n - 1)
-        ]
+    turn_to = 1 - 2 * lax.rem(line, 2)
+    twin = line + turn_to
+
+    def iterate_copy(turn, src, dst_at, sem_at, peer):
+        return pltpu.make_async_remote_copy(
+            src_ref=src,
+            dst_ref=it_recv.at[turn, dst_at],
+            send_sem=s_sems.at[turn, sem_at],
+            recv_sem=r_sems.at[turn, dst_at],
+            device_id=(peer, col),
+            device_id_type=MESH,
+        )
+
+    twin_at = lax.rem(turn_to + n, n) - 1
+    twin_from = lax.rem(n - turn_to, n) - 1
+
+    def send_iterate(turn):
+        copies = [iterate_copy(turn, it_send.at[turn], twin_at, 0, twin)]
+        for o in range(2, n, 2):
+            copies.append(iterate_copy(turn, it_send.at[turn], o - 1, o - 1, peers[o - 1]))
         for k, side in enumerate((above, below)):
             copies.append(
                 pltpu.make_async_remote_copy(
@@ -131,7 +147,27 @@
                     device_id_type=MESH,
                 )
             )
+        for copy in copies:
+            copy.start()
         return copies
+
+    def take_iterates(turn, copies):
+        passed = []
+        for o in range(2, n, 2):
+            copies[o // 2].wait_recv()
+            dst_at = lax.rem(o + turn_to + n, n) - 1
+            passed.append(iterate_copy(turn, it_recv.at[turn, o - 1], dst_at, o, twin))
+            passed[-1].start()
+        for copy in copies:
+            copy.wait_send()
+        for copy in copies[n // 2 :]:
+            copy.wait_recv()
+        iterate_copy(turn, it_send.at[turn], twin_from, 0, twin).wait_recv()
+        for o in range(2, n, 2):
+            source_at = lax.rem(o - turn_to + n, n) - 1
+            iterate_copy(turn, it_send.at[turn], source_at, o, twin).wait_recv()
+        for copy in passed:
+            copy.wait_send()
 
     row_id = lax.broadcasted_iota(jnp.int32, (8, 128), 0)
 
@@ -188,6 +224,8 @@
         groups(rows, body)
 
     loads[0].wait()
+    pl.semaphore_wait(barrier, n + 1)
+    p_copies = []
     for o in range(n - 1):
 
         def pack(k, carry):
@@ -196,10 +234,8 @@
             return carry
 
         lax.fori_loop(0, cap // 4, pack, 0)
-    pl.semaphore_wait(barrier, n + 1)
-    p_copies = [to_peer(2, o, send_p.at[o], recv_p.at[o]) for o in range(n - 1)]
-    for copy in p_copies:
-        copy.start()
+        p_copies.append(to_peer(2, o, send_p.at[o], recv_p.at[o]))
+        p_copies[-1].start()
 
     loads[1].wait()
 
@@ -209,9 +245,7 @@
 
     groups(rows, first_sweep)
     it_send[0] = iterate[...].astype(BF)
-    it_copies = iterate_copies(0)
-    for copy in it_copies:
-        copy.start()
+    it_copies = send_iterate(0)
 
     loads[2].wait()
     b_copies = []
@@ -229,8 +263,7 @@
 
     for load in loads[3:]:
         load.wait()
-    for copy in it_copies:
-        copy.wait()
+    take_iterates(0, it_copies)
     gather_rows(0)
     subtract_operator()
 
@@ -241,9 +274,7 @@
 
     groups(rows, second_sweep)
     it_send[1] = iterate[...].astype(BF)
-    it_copies = iterate_copies(1)
-    for copy in it_copies:
-        copy.start()
+    it_copies = send_iterate(1)
 
     i_copies = []
     for o in range(n - 1):
@@ -260,8 +291,7 @@
         i_copies.append(to_peer(4, o, send_i.at[o], recv_i.at[o]))
         i_copies[-1].start()
 
-    for copy in it_copies:
-        copy.wait()
+    take_iterates(1, it_copies)
     gather_rows(1)
     subtract_operator()
 
@@ -371,21 +401,10 @@
     store.wait()
 
 
-def hand_over(fine, blocks, rest, fine_out, blocks_out, rest_out, sems):
-    count = sems.shape[0] - 2
-    size = blocks.shape[0] // count
-    copies = [
-        pltpu.make_async_copy(
-            blocks.at[pl.ds(k * size, size)], blocks_out.at[pl.ds(k * size, size)], sems.at[k]
-        )
-        for k in range(count)
-    ]
-    copies.append(pltpu.make_async_copy(fine, fine_out, sems.at[count]))
-    copies.append(pltpu.make_async_copy(rest, rest_out, sems.at[count + 1]))
-    for copy in copies:
-        copy.start()
-    for copy in copies:
-        copy.wait()
+def hand_over(fine, blocks, rest, fine_out, blocks_out, rest_out):
+    fine_out[...] = fine[...]
+    blocks_out[...] = blocks[...]
+    rest_out[...] = rest[...]
 
 
 def tables(n, m, cap, rows, col_index, partner, odd_owner):
@@ -474,8 +493,8 @@
             slot_vals,
             slot_vals,
             dma((6,)),
-            dma((7, n - 1)),
-            dma((7, n - 1)),
+            dma((7, n)),
+            dma((7, n)),
             dma((2, 2)),
             dma((2, 2)),
         ],
@@ -483,12 +502,19 @@
             collective_id=0, has_side_effects=True, vmem_limit_bytes=61 * 1024 * 1024
         ),
     )(idx, rhs, a_diag, a_pair, a_far, approx_inv, prolong)
+    steps = 4
+    parts = [
+        pl.BlockSpec((rows // steps, width), lambda i: (i, 0)),
+        pl.BlockSpec((half // steps,) + block, lambda i: (i, 0, 0)),
+        pl.BlockSpec((half // steps, width), lambda i: (i, 0)),
+    ]
     return pl.pallas_call(
         hand_over,
+        grid=(steps,),
         out_shape=[jax.ShapeDtypeStruct(a.shape, a.dtype) for a in (fine, blocks, restricted)],
-        in_specs=[hbm] * 3,
-        out_specs=[hbm] * 3,
-        scratch_shapes=[dma((10,))],
+        in_specs=parts,
+        out_specs=parts,
+        compiler_params=pltpu.CompilerParams(vmem_limit_bytes=16 * 1024 * 1024),
     )(fine, blocks, restricted)
 
 

time: 233 us -> 167 us (0.72)
  Pallas kernels: 227 us -> 158 us
  local copies, waits for them, and re-layouts: 0.91 us -> 4.09 us
    pallas_call x1, Pallas kernels: 67.7 us -> 1.84 us  [body(): pl.pallas_call(hand_over, grid=(steps,), out_shape=[jax.ShapeDtypeStruct(...]
    unnamed x0 -> x6, local copies, waits for them, and re-layouts: none -> 3.18 us
    pallas_call x1, Pallas kernels: 159 us -> 157 us  [body(): pl.pallas_call(functools.partial(kernel, n, m, cap, rows), out_shape=(jax...]
where the time goes in v3:
time: 167 us
  Pallas kernels  158 us (95%)
  local copies, waits for them, and re-layouts  4.09 us (2%)
  other arithmetic  3.47 us (2%)
    pallas_call x1, Pallas kernels, body(): pl.pallas_call(functools.partial(kernel, n, m, cap, rows), out_shape=(jax...  157 us

profile of v3, /device:TPU:0, one launch (start us, length us, event | category | flops | bytes accessed | tf_op | source)
XLA Modules:
  0.0 166.6 jit_solution(10064827357588745073)
XLA Ops:
  0.7 0.8 fusion.3
  1.4 0.7 and_select_fusion
  2.1 0.7 pad_add_fusion
  2.8 0.9 convert_reduce_fusion
  3.7 0.1 select_reduce_fusion.1
  3.8 0.2 convert_reduce_fusion.1
  4.0 0.1 select_reduce_fusion
  4.1 0.1 copy.14
  4.2 0.1 reshape.17
  4.4 0.7 concatenate.3.idx
  5.1 156.5 %shard_map.112 = (f32[128,128]{1,0:T(8,128)}, bf16[64,128,128]{2,1,0:T(8,128)(2,1)}, f32[64,128]{1,0:T(8,128)}) custom-call(s32[736]{0:T(1024)} %concatenate.3.idx, f32[128,128]{1,0:T(8,128)} %rhs.1, bf16[128,128,128]{2,1,0:T(8,128)(2,1)} %h_diag.1, bf16[128,128,128]{2,1,0:T(8,128)(2,1)} %h_pair.1, bf16[128,2,128,128]{3,2,1,0:T(8,128)(2,1)} %h_far.1, ...), custom_call_target="tpu_custom_call" | custom-call | tf_op jit(solution)/shard_map/pallas_call | solution.py:455
  161.6 0.0 copy-start
  161.6 1.6 copy-done
  163.2 0.0 copy-start.1
  163.2 0.8 copy-done.1
  164.0 0.0 copy-start.2
  164.0 0.8 copy-done.2
  164.8 1.8 %shard_map.113 = (f32[128,128]{1,0:T(8,128)}, bf16[64,128,128]{2,1,0:T(8,128)(2,1)}, f32[64,128]{1,0:T(8,128)}) custom-call(f32[128,128]{1,0:T(8,128)S(1)} %copy-done.1, bf16[64,128,128]{2,1,0:T(8,128)(2,1)S(1)} %copy-done, f32[64,128]{1,0:T(8,128)S(1)} %copy-done.2), custom_call_target="tpu_custom_call" | custom-call | tf_op jit(solution)/shard_map/pallas_call | solution.py:511
  (3 shorter events, 0.0 us)
Async XLA Ops:
  161.6 1.6 copy-start
  163.2 0.8 copy-start.1
  164.0 0.8 copy-start.2

commit v4 on v3

--- a/solution.py
+++ b/solution.py
@@ -195,7 +195,7 @@
         def step(g, carry):
             for r in range(8):
                 i = g * 8 + r
-                a = idx[mate_at + i]
+                a = idx[mate_at + (r % 2) * half + g * 4 + r // 2]
                 b = idx[far_at + i]
                 c = idx[side_at + i]
                 mate_rows[pl.ds(i, 1), :] = line_vals[a // rows, pl.ds(a % rows, 1), :]
@@ -412,7 +412,6 @@
     slots = (n - 1) * cap
     line = lax.axis_index("rx")
     col = lax.axis_index("ry")
-    mate = jnp.stack([partner, 2 * odd_owner], axis=1).reshape(rows)
 
     def line_slot(row):
         return (line - row // rows // m) % n * rows + row % rows
@@ -434,7 +433,16 @@
         return jnp.sum(jnp.where(hits, order[None, :], 0), axis=1, dtype=jnp.int32)
 
     return jnp.concatenate(
-        [line_slot(mate), line_slot(col_index[:, 0]), side, recv, send, inverse(send), inverse(recv)]
+        [
+            line_slot(partner),
+            line_slot(2 * odd_owner),
+            line_slot(col_index[:, 0]),
+            side,
+            recv,
+            send,
+            inverse(send),
+            inverse(recv),
+        ]
     )
 
 
@@ -514,7 +522,7 @@
         out_shape=[jax.ShapeDtypeStruct(a.shape, a.dtype) for a in (fine, blocks, restricted)],
         in_specs=parts,
         out_specs=parts,
-        compiler_params=pltpu.CompilerParams(vmem_limit_bytes=16 * 1024 * 1024),
+        compiler_params=pltpu.CompilerParams(vmem_limit_bytes=61 * 1024 * 1024),
     )(fine, blocks, restricted)
 
 

time: 167 us -> 165 us (0.988)
  local copies, waits for them, and re-layouts: 4.09 us -> 0.67 us
  Pallas kernels: 158 us -> 160 us
    unnamed x6 -> x0, local copies, waits for them, and re-layouts: 3.18 us -> none
    pallas_call x1, Pallas kernels: 1.84 us -> 3.8 us  [body(): pl.pallas_call(hand_over, grid=(steps,), out_shape=[jax.ShapeDtypeStruct(...]
where the time goes in v4:
time: 165 us; the launch traced here: 164 us
  Pallas kernels  160 us (97%)
  other arithmetic  2.79 us (2%)
    pallas_call x1, Pallas kernels, body(): pl.pallas_call(functools.partial(kernel, n, m, cap, rows), out_shape=(jax...  157 us
    pallas_call x1, Pallas kernels, body(): pl.pallas_call(hand_over, grid=(steps,), out_shape=[jax.ShapeDtypeStruct(...  3.8 us

profile of v4, /device:TPU:0, one launch (start us, length us, event | category | flops | bytes accessed | tf_op | source)
XLA Modules:
  0.0 164.5 jit_solution(16466246611103718527)
XLA Ops:
  0.7 0.8 fusion.4
  1.4 0.7 and_select_fusion
  2.1 0.9 convert_reduce_fusion
  3.1 0.1 select_reduce_fusion.1
  3.2 0.2 convert_reduce_fusion.1
  3.4 0.1 select_reduce_fusion
  3.5 0.7 concatenate.3.idx
  4.1 156.5 %shard_map.112 = (f32[128,128]{1,0:T(8,128)}, bf16[64,128,128]{2,1,0:T(8,128)(2,1)}, f32[64,128]{1,0:T(8,128)}) custom-call(s32[736]{0:T(1024)} %concatenate.3.idx, f32[128,128]{1,0:T(8,128)} %rhs.1, bf16[128,128,128]{2,1,0:T(8,128)(2,1)} %h_diag.1, bf16[128,128,128]{2,1,0:T(8,128)(2,1)} %h_pair.1, bf16[128,2,128,128]{3,2,1,0:T(8,128)(2,1)} %h_far.1, ...), custom_call_target="tpu_custom_call" | custom-call | tf_op jit(solution)/shard_map/pallas_call | solution.py:463
  160.7 3.8 %shard_map.113 = (f32[128,128]{1,0:T(8,128)}, bf16[64,128,128]{2,1,0:T(8,128)(2,1)}, f32[64,128]{1,0:T(8,128)}) custom-call(f32[128,128]{1,0:T(8,128)} %get-tuple-element.6.fine, bf16[64,128,128]{2,1,0:T(8,128)(2,1)} %get-tuple-element.7.blocks, f32[64,128]{1,0:T(8,128)} %get-tuple-element.8.rest), custom_call_target="tpu_custom_call" | custom-call | tf_op jit(solution)/shard_map/pallas_call | solution.py:519
  (2 shorter events, 0.0 us)
